TPU v7x, 32 devices: a whole 2x2x4 slice. The times are simulated.
32 devices in a mesh: occ: 4 (over y, core), vir: 8 (over z, x).
Axes of the slice: x: 2, y: 2, z: 4, core: 2. Of those that a mesh axis runs over, the one named last changes fastest.
Arguments:
- amplitudes: bfloat16 [2304, 8192], P('occ', 'vir'), may hold values from -6 to 6
- integrals: bfloat16 [8, 8, 1024, 1024], P('vir'), may hold values from -0.0625 to 0.0625
- cd_tiles: int32 [8, 8], P('vir'), may hold values from 0 to 7, as said below
- cd_count: int32 [8], P('vir'), may hold values from 1 to 8, as said below
Outputs:
- residual: bfloat16 [2304, 8192], P('occ', 'vir')
Inputs may be any that keep to these rules, and one draw needn't show every extreme that they name: `cd_tiles`: entries of one row are distinct and the first is the row's own pair tile. `cd_count`: slots at or past the count are unused.
All inputs are finite; a program needn't handle non-finite values.
Results may differ from a plain program's by a relative error of at most 0.0075.
Values may be sent and summed in bfloat16 or wider, within the bound.
A program may use at most 128 MiB of HBM per device.

v0:
```python
import jax
import jax.numpy as jnp
from jax import lax
from jax.sharding import PartitionSpec as P

TW = 32
K = 1024
OCC_DEV = 12
CD_MAX = 8


def swapped(shard, axis, apart):
    return lax.ppermute(shard, axis, [(i, i ^ 1 << apart) for i in range(lax.axis_size(axis))])


def reflect_rows(matrix):
    occ_devices = lax.axis_size("occ")
    reshaped = matrix.reshape(OCC_DEV, occ_devices, OCC_DEV, matrix.shape[1])
    arrived = lax.all_to_all(reshaped, "occ", split_axis=1, concat_axis=1, tiled=True)
    return arrived.transpose(2, 1, 0, 3).reshape(matrix.shape)


def reflect_tiles(matrix):
    arrived = swapped(matrix, "vir", 0)
    row_count = matrix.shape[0]
    return arrived.reshape(row_count, TW, TW).transpose(0, 2, 1).reshape(row_count, K)


def on_device(amplitudes, integrals, cd_tiles, cd_count):
    row_count = amplitudes.shape[0]
    listed = cd_tiles[0]
    live_count = cd_count[0]
    blocks = integrals[0]
    zero_block = jnp.zeros((row_count, K), jnp.float32)

    def product(col_tile, slot_index):
        int_block = lax.dynamic_index_in_dim(blocks, slot_index, 0, keepdims=False)
        return lax.dot_general(
            col_tile, int_block, (((1,), (1,)), ((), ())), preferred_element_type=jnp.float32
        )

    gathered = lax.all_gather(amplitudes, "vir", axis=1, tiled=True)

    def visit_slot(slot_pos, running):
        tile_id = listed[slot_pos]

        def apply_block(current):
            col_tile = lax.dynamic_slice_in_dim(gathered, tile_id * K, K, 1)
            return current + product(col_tile, slot_pos)

        return lax.cond(slot_pos < live_count, apply_block, lambda current: current, running)

    ladder = lax.fori_loop(0, CD_MAX, visit_slot, zero_block)
    ladder = ladder.astype(jnp.bfloat16)
    mirrored = reflect_tiles(reflect_rows(ladder))
    summed = ladder.astype(jnp.float32) + mirrored.astype(jnp.float32)
    return summed.astype(jnp.bfloat16)


def solution(mesh):
    placed = (P("occ", "vir"), P("vir", None, None, None), P("vir", None), P("vir"))
    return jax.shard_map(
        on_device, mesh=mesh, in_specs=placed, out_specs=P("occ", "vir"), check_vma=False
    )
```

profile of v0, /device:TPU:0, one launch (start us, length us, event | category | flops | bytes accessed | tf_op | source)
XLA Modules:
  0.0 271.6 jit_solution(486228156846691606)
XLA Ops:
  7.3 143.1 %all-gather.2.cloned.1.call-done = bf16[576,8192]{1,0:T(8,128)(2,1)} async-done(((bf16[576,1024]{1,0:T(8,128)(2,1)}), bf16[576,8192]{1,0:T(8,128)(2,1)}) %all-gather.2.cloned.1.call-update) | async-done | bytes 9437200 | tf_op jit(solution)/shard_map/all_gather | solution.py:42
  150.6 39.4 %while.16 = (s32[]{:T(128)}, f32[576,1024]{1,0:T(8,128)S(1)}, s32[]{:T(128)}, s32[8]{0:T(128)S(1)}, bf16[576,8192]{1,0:T(8,128)(2,1)}, /*index=5*/bf16[8,1024,1024]{2,1,0:T(8,128)(2,1)}, s32[]{:T(128)}) while((s32[]{:T(128)}, f32[576,1024]{1,0:T(8,128)S(1)}, s32[]{:T(128)}, s32[8]{0:T(128)S(1)}, bf16[576,8192]{1,0:T(8,128)(2,1)}, ...), condition=%wide.region_3.4_spmd, body=%wide.region_0.3_spmd.sunk | while | flops 1208549376 | bytes 7995631 | solution.py:53
  151.3 4.9 %conditional.2 = (f32[576,1024]{1,0:T(8,128)S(1)}) conditional(s32[]{:T(128)} %convert_element_type.42, f32[576,1024]{1,0:T(8,128)S(1)} %get-tuple-element.236, (s32[]{:T(128)}, s32[8]{0:T(128)S(1)}, bf16[576,8192]{1,0:T(8,128)(2,1)}, bf16[8,1024,1024]{2,1,0:T(8,128)(2,1)}, f32[576,1024]{1,0:T(8,128)S(1)}) %tuple.45), branch_computations={%region_1.0_spmd, %region_2.2_spmd} | conditional | flops 1208549376 | bytes 7995500 | solution.py:51
  152.6 3.6 %fusion.3 = f32[576,1024]{1,0:T(8,128)S(1)} fusion(f32[576,1024]{1,0:T(8,128)S(1)} %get-tuple-element.165, bf16[8,1024,1024]{2,1,0:T(8,128)(2,1)} %get-tuple-element.169, s32[]{:T(128)S(6)} %select_n.18, bf16[576,8192]{1,0:T(8,128)(2,1)} %get-tuple-element.166, s32[]{:T(128)S(6)} %select_n.19), kind=kOutput, calls=%fused_computation.3 | convolution fusion | flops 1208549376 | bytes 7995400 | tf_op jit(solution)/shard_map/while/body/eval_jaxpr/cond/branch_1_fun/dot_general | solution.py:38
  156.8 4.9 %conditional.2 = (f32[576,1024]{1,0:T(8,128)S(1)}) conditional(s32[]{:T(128)} %convert_element_type.42, f32[576,1024]{1,0:T(8,128)S(1)} %get-tuple-element.236, (s32[]{:T(128)}, s32[8]{0:T(128)S(1)}, bf16[576,8192]{1,0:T(8,128)(2,1)}, bf16[8,1024,1024]{2,1,0:T(8,128)(2,1)}, f32[576,1024]{1,0:T(8,128)S(1)}) %tuple.45), branch_computations={%region_1.0_spmd, %region_2.2_spmd} | conditional | flops 1208549376 | bytes 7995500 | solution.py:51
  158.1 3.6 %fusion.3 = f32[576,1024]{1,0:T(8,128)S(1)} fusion(f32[576,1024]{1,0:T(8,128)S(1)} %get-tuple-element.165, bf16[8,1024,1024]{2,1,0:T(8,128)(2,1)} %get-tuple-element.169, s32[]{:T(128)S(6)} %select_n.18, bf16[576,8192]{1,0:T(8,128)(2,1)} %get-tuple-element.166, s32[]{:T(128)S(6)} %select_n.19), kind=kOutput, calls=%fused_computation.3 | convolution fusion | flops 1208549376 | bytes 7995400 | tf_op jit(solution)/shard_map/while/body/eval_jaxpr/cond/branch_1_fun/dot_general | solution.py:38
  162.4 4.9 %conditional.2 = (f32[576,1024]{1,0:T(8,128)S(1)}) conditional(s32[]{:T(128)} %convert_element_type.42, f32[576,1024]{1,0:T(8,128)S(1)} %get-tuple-element.236, (s32[]{:T(128)}, s32[8]{0:T(128)S(1)}, bf16[576,8192]{1,0:T(8,128)(2,1)}, bf16[8,1024,1024]{2,1,0:T(8,128)(2,1)}, f32[576,1024]{1,0:T(8,128)S(1)}) %tuple.45), branch_computations={%region_1.0_spmd, %region_2.2_spmd} | conditional | flops 1208549376 | bytes 7995500 | solution.py:51
  163.7 3.6 %fusion.3 = f32[576,1024]{1,0:T(8,128)S(1)} fusion(f32[576,1024]{1,0:T(8,128)S(1)} %get-tuple-element.165, bf16[8,1024,1024]{2,1,0:T(8,128)(2,1)} %get-tuple-element.169, s32[]{:T(128)S(6)} %select_n.18, bf16[576,8192]{1,0:T(8,128)(2,1)} %get-tuple-element.166, s32[]{:T(128)S(6)} %select_n.19), kind=kOutput, calls=%fused_computation.3 | convolution fusion | flops 1208549376 | bytes 7995400 | tf_op jit(solution)/shard_map/while/body/eval_jaxpr/cond/branch_1_fun/dot_general | solution.py:38
  167.9 4.9 %conditional.2 = (f32[576,1024]{1,0:T(8,128)S(1)}) conditional(s32[]{:T(128)} %convert_element_type.42, f32[576,1024]{1,0:T(8,128)S(1)} %get-tuple-element.236, (s32[]{:T(128)}, s32[8]{0:T(128)S(1)}, bf16[576,8192]{1,0:T(8,128)(2,1)}, bf16[8,1024,1024]{2,1,0:T(8,128)(2,1)}, f32[576,1024]{1,0:T(8,128)S(1)}) %tuple.45), branch_computations={%region_1.0_spmd, %region_2.2_spmd} | conditional | flops 1208549376 | bytes 7995500 | solution.py:51
  169.2 3.6 %fusion.3 = f32[576,1024]{1,0:T(8,128)S(1)} fusion(f32[576,1024]{1,0:T(8,128)S(1)} %get-tuple-element.165, bf16[8,1024,1024]{2,1,0:T(8,128)(2,1)} %get-tuple-element.169, s32[]{:T(128)S(6)} %select_n.18, bf16[576,8192]{1,0:T(8,128)(2,1)} %get-tuple-element.166, s32[]{:T(128)S(6)} %select_n.19), kind=kOutput, calls=%fused_computation.3 | convolution fusion | flops 1208549376 | bytes 7995400 | tf_op jit(solution)/shard_map/while/body/eval_jaxpr/cond/branch_1_fun/dot_general | solution.py:38
  173.4 4.9 %conditional.2 = (f32[576,1024]{1,0:T(8,128)S(1)}) conditional(s32[]{:T(128)} %convert_element_type.42, f32[576,1024]{1,0:T(8,128)S(1)} %get-tuple-element.236, (s32[]{:T(128)}, s32[8]{0:T(128)S(1)}, bf16[576,8192]{1,0:T(8,128)(2,1)}, bf16[8,1024,1024]{2,1,0:T(8,128)(2,1)}, f32[576,1024]{1,0:T(8,128)S(1)}) %tuple.45), branch_computations={%region_1.0_spmd, %region_2.2_spmd} | conditional | flops 1208549376 | bytes 7995500 | solution.py:51
  174.7 3.6 %fusion.3 = f32[576,1024]{1,0:T(8,128)S(1)} fusion(f32[576,1024]{1,0:T(8,128)S(1)} %get-tuple-element.165, bf16[8,1024,1024]{2,1,0:T(8,128)(2,1)} %get-tuple-element.169, s32[]{:T(128)S(6)} %select_n.18, bf16[576,8192]{1,0:T(8,128)(2,1)} %get-tuple-element.166, s32[]{:T(128)S(6)} %select_n.19), kind=kOutput, calls=%fused_computation.3 | convolution fusion | flops 1208549376 | bytes 7995400 | tf_op jit(solution)/shard_map/while/body/eval_jaxpr/cond/branch_1_fun/dot_general | solution.py:38
  179.0 4.9 %conditional.2 = (f32[576,1024]{1,0:T(8,128)S(1)}) conditional(s32[]{:T(128)} %convert_element_type.42, f32[576,1024]{1,0:T(8,128)S(1)} %get-tuple-element.236, (s32[]{:T(128)}, s32[8]{0:T(128)S(1)}, bf16[576,8192]{1,0:T(8,128)(2,1)}, bf16[8,1024,1024]{2,1,0:T(8,128)(2,1)}, f32[576,1024]{1,0:T(8,128)S(1)}) %tuple.45), branch_computations={%region_1.0_spmd, %region_2.2_spmd} | conditional | flops 1208549376 | bytes 7995500 | solution.py:51
  180.3 3.6 %fusion.3 = f32[576,1024]{1,0:T(8,128)S(1)} fusion(f32[576,1024]{1,0:T(8,128)S(1)} %get-tuple-element.165, bf16[8,1024,1024]{2,1,0:T(8,128)(2,1)} %get-tuple-element.169, s32[]{:T(128)S(6)} %select_n.18, bf16[576,8192]{1,0:T(8,128)(2,1)} %get-tuple-element.166, s32[]{:T(128)S(6)} %select_n.19), kind=kOutput, calls=%fused_computation.3 | convolution fusion | flops 1208549376 | bytes 7995400 | tf_op jit(solution)/shard_map/while/body/eval_jaxpr/cond/branch_1_fun/dot_general | solution.py:38
  184.5 4.9 %conditional.2 = (f32[576,1024]{1,0:T(8,128)S(1)}) conditional(s32[]{:T(128)} %convert_element_type.42, f32[576,1024]{1,0:T(8,128)S(1)} %get-tuple-element.236, (s32[]{:T(128)}, s32[8]{0:T(128)S(1)}, bf16[576,8192]{1,0:T(8,128)(2,1)}, bf16[8,1024,1024]{2,1,0:T(8,128)(2,1)}, f32[576,1024]{1,0:T(8,128)S(1)}) %tuple.45), branch_computations={%region_1.0_spmd, %region_2.2_spmd} | conditional | flops 1208549376 | bytes 7995500 | solution.py:51
  185.8 3.6 %fusion.3 = f32[576,1024]{1,0:T(8,128)S(1)} fusion(f32[576,1024]{1,0:T(8,128)S(1)} %get-tuple-element.165, bf16[8,1024,1024]{2,1,0:T(8,128)(2,1)} %get-tuple-element.169, s32[]{:T(128)S(6)} %select_n.18, bf16[576,8192]{1,0:T(8,128)(2,1)} %get-tuple-element.166, s32[]{:T(128)S(6)} %select_n.19), kind=kOutput, calls=%fused_computation.3 | convolution fusion | flops 1208549376 | bytes 7995400 | tf_op jit(solution)/shard_map/while/body/eval_jaxpr/cond/branch_1_fun/dot_general | solution.py:38
  193.1 22.6 %all_to_all.5 = bf16[12,4,12,1024]{3,2,0,1:T(8,128)(2,1)S(1)} all-to-all(bf16[12,4,12,1024]{3,2,0,1:T(8,128)(2,1)S(1)} %copy.18), channel_id=1, replica_groups=mesh['occ'=4,'vir'=8] {'occ'}, dimensions={1} | all-to-all | bytes 2359296 | tf_op jit(solution)/shard_map/all_to_all | solution.py:19
  217.6 2.2 reshape.15
  219.8 5.5 %collective-permute-start = (bf16[576,1024]{1,0:T(8,128)(2,1)S(1)}, bf16[576,1024]{1,0:T(8,128)(2,1)}, u32[]{:S(2)}, u32[]{:S(2)}) collective-permute-start(bf16[576,1024]{1,0:T(8,128)(2,1)S(1)} %reshape.15), channel_id=1, source_target_pairs={{0,1},{1,0},{2,3},{3,2},{4,5},{5,4},{6,7},{7,6},{8,9},{9,8},{10,11... | collective-permute-start | bytes 3538952 | tf_op jit(solution)/shard_map/ppermute | solution.py:13
  225.3 25.7 %collective-permute-done = bf16[576,1024]{1,0:T(8,128)(2,1)} collective-permute-done((bf16[576,1024]{1,0:T(8,128)(2,1)S(1)}, bf16[576,1024]{1,0:T(8,128)(2,1)}, u32[]{:S(2)}, u32[]{:S(2)}) %collective-permute-start) | collective-permute-done | bytes 1179680 | tf_op jit(solution)/shard_map/ppermute | solution.py:13
  251.0 2.8 %copy.20 = f32[576,1024]{0,1:T(8,128)} copy(bf16[576,1024]{1,0:T(8,128)(2,1)} %collective-permute-done) | data formatting | bytes 3538944 | tf_op jit(solution)/shard_map/convert_element_type | solution.py:56
  253.8 4.8 %copy.21 = f32[576,32,32]{0,2,1:T(8,128)} copy(f32[576,32,32]{0,1,2:T(8,128)} %bitcast.14) | data formatting | bytes 4718592 | tf_op jit(solution)/shard_map/convert_element_type | solution.py:56
  258.6 3.1 %copy.22 = f32[576,1024]{1,0:T(8,128)} copy(f32[576,1024]{0,1:T(8,128)} %bitcast.15) | data formatting | bytes 4718592 | tf_op jit(solution)/shard_map/convert_element_type | solution.py:56
  261.7 3.0 %add_convert_fusion = bf16[576,1024]{1,0:T(8,128)(2,1)} fusion(f32[576,1024]{1,0:T(8,128)} %copy.22, f32[576,1024]{1,0:T(8,128)S(1)} %get-tuple-element.178), kind=kLoop, calls=%fused_computation.6 | loop fusion | flops 2359296 | bytes 5898240 | tf_op jit(solution)/shard_map/convert_element_type | solution.py:57
  (17 shorter events, 10.3 us)
Async XLA Ops:
  6.5 144.1 %copy-start = (s32[1,8]{1,0:T(1,128)S(1)}, s32[1,8]{1,0:T(1,128)}, u32[]{:S(2)}) copy-start(s32[1,8]{1,0:T(1,128)} %param.10) | copy-start | bytes 100
  6.5 143.8 %all-gather.2.cloned.1.call-start = ((), (), s32[]{:S(2)}) async-start(), calls=%async_computation.1 | async-start | bytes 10616832 | tf_op jit(solution)/shard_map/all_gather | solution.py:42
  219.8 31.2 %collective-permute-start = (bf16[576,1024]{1,0:T(8,128)(2,1)S(1)}, bf16[576,1024]{1,0:T(8,128)(2,1)}, u32[]{:S(2)}, u32[]{:S(2)}) collective-permute-start(bf16[576,1024]{1,0:T(8,128)(2,1)S(1)} %reshape.15), channel_id=1, source_target_pairs={{0,1},{1,0},{2,3},{3,2},{4,5},{5,4},{6,7},{7,6},{8,9},{9,8},{10,11... | collective-permute-start | bytes 3538952 | tf_op jit(solution)/shard_map/ppermute | solution.py:13
Sparse Core Ops, SparseCore 0:
  9.5 140.7 all-gather.1
where the time goes:
time: 273 us; the launch traced here: 272 us
  waiting for transfers between devices  169 us (62%)
  matrix products  24.9 us (9%)
  blocking collectives  22.6 us (8%)
  local copies, waits for them, and re-layouts  22.4 us (8%)
  between operations  13.4 us (5%)
  loops' own time  10 us (4%)
  starting transfers between devices  5.48 us (2%)
  other arithmetic  3.23 us (1%)
    all_gather x1, waiting for transfers between devices, on_device(): gathered = lax.all_gather(amplitudes, 'vir', axis=1, tiled=True)  143 us
    ppermute x1, waiting for transfers between devices, swapped(): lax.ppermute(shard, axis, [(i, i ^ 1 << apart) for i in range(lax.axis_si...  25.7 us
    dot_general x7, matrix products, product(): lax.dot_general(col_tile, int_block, (((1,), (1,)), ((), ())), preferred_...  24.9 us
    all_to_all x1, blocking collectives, reflect_rows(): lax.all_to_all(reshaped, 'occ', split_axis=1, concat_axis=1, tiled=True)  22.6 us
    convert_element_type x3, local copies, waits for them, and re-layouts, on_device(): summed = ladder.astype(jnp.float32) + mirrored.astype(jnp.float32)  10.7 us
    ppermute x1, starting transfers between devices, swapped(): lax.ppermute(shard, axis, [(i, i ^ 1 << apart) for i in range(lax.axis_si...  5.48 us
  transfers between devices with their start and end apart: 2, of which 2 were waited for; matrix products, arithmetic and copies ran while one was open for 0% of the time, Pallas kernels for 0%

commit v1 on v0

v1 whole, which is shorter than its diff:
```python
import functools
import math

import jax
import jax.numpy as jnp
from jax import lax
from jax.experimental import pallas as pl
from jax.experimental.pallas import tpu as pltpu
from jax.sharding import PartitionSpec as P

VMEM_BYTES = 52 * 2**20
COLS = 256
MESH = pl.DeviceIdType.MESH
X_FIRST = 1


def select(table, at):
    found = jnp.int32(table[0])
    for pos in range(1, len(table)):
        found = jnp.where(at == pos, jnp.int32(table[pos]), found)
    return found


def ladder_kernel(n_occ, n_vir, slot_ref, amp_ref, int_hbm, out_ref,
                  gath, ints, turn, flip, lad, mir, acc,
                  int_sem, send_sem, recv_sem, swap_send, swap_recv):
    n_line = n_vir // 2
    n_blocks, cd_max = n_occ, int_hbm.shape[0]
    rows, k = amp_ref.shape[1:]
    width, side = math.isqrt(k), math.isqrt(rows)
    occ, vir = lax.axis_index("occ"), lax.axis_index("vir")
    line, pair = vir // 2, vir % 2
    partner = line * 2 + 1 - pair

    near = [sorted(range(n_line), key=lambda at: (abs(at - here), at)) for here in range(n_line)]
    by_rank = [select([near[here][rank] for here in range(n_line)], line) for rank in range(n_line)]

    def block_of(step):
        flipped = n_blocks - 1 - step
        out, bit = 0, 1
        while bit < n_blocks:
            out = out + bit * (((occ // bit) % 2 + (flipped // bit) % 2) % 2)
            bit *= 2
        return out

    barrier = pltpu.get_barrier_semaphore()

    @pl.when(line > 0)
    def _():
        pl.semaphore_signal(barrier, inc=1, device_id=(occ, vir - 2), device_id_type=MESH)

    @pl.when(line < n_line - 1)
    def _():
        pl.semaphore_signal(barrier, inc=1, device_id=(occ, vir + 2), device_id_type=MESH)

    for other in range(n_occ):
        pl.semaphore_signal(barrier, inc=1, device_id=(other, partner), device_id_type=MESH)

    fetch = pltpu.make_async_copy(int_hbm, ints.at[pl.ds(0, cd_max)], int_sem)
    fetch.start()
    for step in range(n_blocks):
        gath[step, vir] = amp_ref[block_of(step)]
    waits = n_occ + jnp.where(line > 0, 1, 0) + jnp.where(line < n_line - 1, 1, 0)
    pl.semaphore_wait(barrier, waits)

    def copies(step, at, own_column):
        tile = at * 2 + (pair if own_column else 1 - pair)
        crossed = step == X_FIRST
        up = (at <= line) & (line < n_line - 1)
        down = (at >= line) & (line > 0)
        if own_column:
            across = jnp.logical_not(crossed) | (at == line)
        else:
            up, down, across = up & crossed, down & crossed, None
        plan = [(0, up, vir + 2), (1, down, vir - 2), (2, across, partner)]

        def copy(way, target):
            return pltpu.make_async_remote_copy(
                src_ref=gath.at[step, tile],
                dst_ref=gath.at[step, tile],
                send_sem=send_sem.at[way, step, tile],
                recv_sem=recv_sem.at[step, tile],
                device_id=(occ, target),
                device_id_type=MESH,
            )

        return [(cond, functools.partial(copy, way, target))
                for way, cond, target in plan if cond is not None]

    def forward(step, at, own_column):
        for cond, make in copies(step, at, own_column):
            @pl.when(cond)
            def _(make=make):
                make().start()

    def arrived(step, at, own_column):
        tile = at * 2 + (pair if own_column else 1 - pair)
        pltpu.make_async_remote_copy(
            src_ref=gath.at[step, tile], dst_ref=gath.at[step, tile],
            send_sem=send_sem.at[0, step, tile], recv_sem=recv_sem.at[step, tile],
            device_id=(occ, partner), device_id_type=MESH,
        ).wait_recv()

    def product(step, at, own_column, first):
        tile = at * 2 + (pair if own_column else 1 - pair)
        slot = slot_ref[tile]

        def part(n, carry):
            cols = pl.ds(pl.multiple_of(n * COLS, COLS), COLS)
            term = lax.dot_general(
                gath[step, tile], ints[slot, cols, :], (((1,), (1,)), ((), ())),
                preferred_element_type=jnp.float32)
            if first:
                acc[:, cols] = term
            else:
                acc[:, cols] += term
            return carry

        lax.fori_loop(0, k // COLS, part, 0)

    def swap(step):
        return pltpu.make_async_remote_copy(
            src_ref=lad.at[step], dst_ref=mir.at[step],
            send_sem=swap_send.at[step], recv_sem=swap_recv.at[step],
            device_id=(block_of(step), partner), device_id_type=MESH,
        )

    def finish(step):
        swap(step).wait_recv()
        block = block_of(step)

        def part(n, carry):
            cols = pl.ds(pl.multiple_of(n * COLS, COLS), COLS)
            turned = jnp.dot(mir[step], turn[:, cols], preferred_element_type=jnp.float32)
            mirrored = jnp.dot(flip[...], turned.astype(jnp.bfloat16), preferred_element_type=jnp.float32)
            out_ref[block, :, cols] = (lad[step, :, cols].astype(jnp.float32) + mirrored).astype(out_ref.dtype)
            return carry

        lax.fori_loop(0, k // COLS, part, 0)

    forward(0, line, True)
    ints[cd_max] = jnp.zeros((k, k), jnp.bfloat16)

    def build(n, carry):
        cols = pl.ds(pl.multiple_of(n * COLS, COLS), COLS)
        row = lax.broadcasted_iota(jnp.int32, (k, COLS), 0)
        col = lax.broadcasted_iota(jnp.int32, (k, COLS), 1) + n * COLS
        turn[:, cols] = jnp.where(row == (col % width) * width + col // width, 1.0, 0.0).astype(jnp.bfloat16)
        return carry

    lax.fori_loop(0, k // COLS, build, 0)
    row = lax.broadcasted_iota(jnp.int32, (rows, rows), 0)
    col = lax.broadcasted_iota(jnp.int32, (rows, rows), 1)
    flip[...] = jnp.where(row == (col % side) * side + col // side, 1.0, 0.0).astype(jnp.bfloat16)
    fetch.wait()

    order = [(0, True)]
    for rank in range(1, n_line):
        order += [(rank, True), (rank - 1, False)]
    order.append((n_line - 1, False))

    def visit(step, carry):
        @pl.when(step + 1 < n_blocks)
        def _():
            forward(step + 1, line, True)

        for number, (rank, own_column) in enumerate(order):
            at = by_rank[rank]
            if number:
                arrived(step, at, own_column)
                forward(step, at, own_column)
            product(step, at, own_column, number == 0)
        lad[step] = acc[...].astype(jnp.bfloat16)
        swap(step).start()

        @pl.when(step > 0)
        def _():
            finish(step - 1)

        return carry

    lax.fori_loop(0, n_blocks, visit, 0)
    finish(n_blocks - 1)

    def drain(step, carry):
        for rank, own_column in order:
            for cond, make in copies(step, by_rank[rank], own_column):
                @pl.when(cond)
                def _(make=make):
                    make().wait_send()
        swap(step).wait_send()
        return carry

    lax.fori_loop(0, n_blocks, drain, 0)


def fused(amplitudes, integrals, cd_tiles, cd_count):
    n_occ, n_vir = lax.axis_size("occ"), lax.axis_size("vir")
    rows, k = amplitudes.shape
    cd_max = integrals.shape[1]
    side = math.isqrt(rows // n_occ)
    listed, live = cd_tiles[0], cd_count[0]
    slots = jnp.arange(cd_max, dtype=jnp.int32)
    hit = (listed[None, :] == jnp.arange(n_vir, dtype=jnp.int32)[:, None]) & (slots < live)[None, :]
    slot_of = jnp.min(jnp.where(hit, slots[None, :], cd_max), axis=1).astype(jnp.int32)
    blocks = amplitudes.reshape(side, n_occ, side, k).transpose(1, 0, 2, 3).reshape(n_occ, side * side, k)
    block = side * side
    bf16 = jnp.bfloat16
    result = pl.pallas_call(
        functools.partial(ladder_kernel, n_occ, n_vir),
        out_shape=jax.ShapeDtypeStruct(blocks.shape, bf16),
        in_specs=[
            pl.BlockSpec(memory_space=pltpu.SMEM),
            pl.BlockSpec(memory_space=pltpu.VMEM),
            pl.BlockSpec(memory_space=pl.ANY),
        ],
        out_specs=pl.BlockSpec(memory_space=pltpu.VMEM),
        scratch_shapes=[
            pltpu.VMEM((n_occ, n_vir, block, k), bf16),
            pltpu.VMEM((cd_max + 1, k, k), bf16),
            pltpu.VMEM((k, k), bf16),
            pltpu.VMEM((block, block), bf16),
            pltpu.VMEM((n_occ, block, k), bf16),
            pltpu.VMEM((n_occ, block, k), bf16),
            pltpu.VMEM((block, k), jnp.float32),
            pltpu.SemaphoreType.DMA,
            pltpu.SemaphoreType.DMA((3, n_occ, n_vir)),
            pltpu.SemaphoreType.DMA((n_occ, n_vir)),
            pltpu.SemaphoreType.DMA((n_occ,)),
            pltpu.SemaphoreType.DMA((n_occ,)),
        ],
        compiler_params=pltpu.CompilerParams(
            collective_id=0, has_side_effects=True, vmem_limit_bytes=VMEM_BYTES),
        cost_estimate=pl.CostEstimate(
            flops=2 * rows * k * k * (n_vir + 1), bytes_accessed=2 * cd_max * k * k, transcendentals=0),
    )(slot_of, blocks, integrals[0])
    return result.reshape(n_occ, side, side, k).transpose(1, 0, 2, 3).reshape(rows, k)


def gathered_whole(amplitudes, integrals, cd_tiles, cd_count):
    n_occ = lax.axis_size("occ")
    rows, k = amplitudes.shape
    side, width = math.isqrt(rows // n_occ), math.isqrt(k)
    listed, live, blocks = cd_tiles[0], cd_count[0], integrals[0]
    gathered = lax.all_gather(amplitudes, "vir", axis=1, tiled=True)

    def visit_slot(slot, running):
        def apply_block(current):
            columns = lax.dynamic_slice_in_dim(gathered, listed[slot] * k, k, 1)
            block = lax.dynamic_index_in_dim(blocks, slot, 0, keepdims=False)
            return current + lax.dot_general(
                columns, block, (((1,), (1,)), ((), ())), preferred_element_type=jnp.float32)

        return lax.cond(slot < live, apply_block, lambda current: current, running)

    zero = jnp.zeros((rows, k), jnp.float32)
    ladder = lax.fori_loop(0, blocks.shape[0], visit_slot, zero).astype(jnp.bfloat16)
    swapped = lax.all_to_all(ladder.reshape(side, n_occ, side, k), "occ", split_axis=1, concat_axis=1, tiled=True)
    swapped = swapped.transpose(2, 1, 0, 3).reshape(rows, k)
    swapped = lax.ppermute(swapped, "vir", [(at, at ^ 1) for at in range(lax.axis_size("vir"))])
    mirrored = swapped.reshape(rows, width, width).transpose(0, 2, 1).reshape(rows, k)
    return (ladder.astype(jnp.float32) + mirrored.astype(jnp.float32)).astype(jnp.bfloat16)


def on_device(amplitudes, integrals, cd_tiles, cd_count):
    rows, k = amplitudes.shape
    needed = 2 * (rows * k * (lax.axis_size("vir") + 6) + (integrals.shape[1] + 2) * k * k)
    run = fused if needed < VMEM_BYTES else gathered_whole
    return run(amplitudes, integrals, cd_tiles, cd_count)


def solution(mesh):
    placed = (P("occ", "vir"), P("vir", None, None, None), P("vir", None), P("vir"))
    return jax.shard_map(
        on_device, mesh=mesh, in_specs=placed, out_specs=P("occ", "vir"), check_vma=False
    )
```

time: 273 us -> 159 us (0.58)
  waiting for transfers between devices: 169 us -> 0 us
  Pallas kernels: 0 us -> 150 us
  matrix products: 24.9 us -> 0 us
  blocking collectives: 22.6 us -> 0 us
  local copies, waits for them, and re-layouts: 22.4 us -> 6.97 us
  between operations: 13.4 us -> 0.71 us
  loops' own time: 10 us -> 0 us
  starting transfers between devices: 5.48 us -> 0 us
  other arithmetic: 3.23 us -> 0.13 us
    pallas_call x0 -> x1, Pallas kernels: none -> 150 us  [fused(): pl.pallas_call(functools.partial(ladder_kernel, n_occ, n_vir), out_shape=...]
    all_gather x1 -> x0, waiting for transfers between devices: 143 us -> none  [on_device(): gathered = lax.all_gather(amplitudes, 'vir', axis=1, tiled=True)]
    ppermute x1 -> x0, waiting for transfers between devices: 25.7 us -> none  [swapped(): lax.ppermute(shard, axis, [(i, i ^ 1 << apart) for i in range(lax.axis_si...]
    dot_general x7 -> x0, matrix products: 24.9 us -> none  [product(): lax.dot_general(col_tile, int_block, (((1,), (1,)), ((), ())), preferred_...]
    all_to_all x1 -> x0, blocking collectives: 22.6 us -> none  [reflect_rows(): lax.all_to_all(reshaped, 'occ', split_axis=1, concat_axis=1, tiled=True)]
    convert_element_type x3 -> x0, local copies, waits for them, and re-layouts: 10.7 us -> none  [on_device(): summed = ladder.astype(jnp.float32) + mirrored.astype(jnp.float32)]
    another operation x9 -> x0, loops' own time: 10 us -> none  [the longest x1 5.38 us: on_device(): ladder = lax.fori_loop(0, CD_MAX, visit_slot, zero_block)]
    ppermute x1 -> x0, starting transfers between devices: 5.48 us -> none  [swapped(): lax.ppermute(shard, axis, [(i, i ^ 1 << apart) for i in range(lax.axis_si...]
  transfers between devices with their start and end apart: 2 -> 0, of which waited for: 2 -> 0; matrix products, arithmetic and copies ran while one was open for 0% -> 0% of each run, Pallas kernels for 0% -> 0%
where the time goes in v1:
time: 159 us; the launch traced here: 158 us
  Pallas kernels  150 us (94%)
  local copies, waits for them, and re-layouts  6.97 us (4%)
    pallas_call x1, Pallas kernels, fused(): pl.pallas_call(functools.partial(ladder_kernel, n_occ, n_vir), out_shape=...  150 us
    reshape x2, local copies, waits for them, and re-layouts, fused(): amplitudes.reshape(side, n_occ, side, k).transpose(1, 0, 2, 3)  3.51 us

profile of v1, /device:TPU:0, one launch (start us, length us, event | category | flops | bytes accessed | tf_op | source)
XLA Modules:
  0.0 157.5 jit_solution(17786250661085017623)
XLA Ops:
  0.0 2.1 %reshape.16 = bf16[12,4,12,1024]{3,2,1,0:T(8,128)(2,1)S(1)} reshape(bf16[576,1024]{1,0:T(8,128)(2,1)} %param.4) | data formatting | bytes 2359296 | tf_op jit(solution)/shard_map/reshape | solution.py:206
  2.2 0.9 copy.11
  3.1 0.0 copy-start
  3.1 1.4 copy.12.amp_ref
  5.1 0.0 copy-done
  5.1 0.1 select_reduce_fusion.slot_ref
  5.3 149.7 %shard_map.46 = bf16[4,144,1024]{2,1,0:T(8,128)(2,1)S(1)} custom-call(s32[8]{0:T(128)S(1)} %select_reduce_fusion.slot_ref, bf16[4,144,1024]{2,1,0:T(8,128)(2,1)} %copy.12.amp_ref, bf16[8,1024,1024]{2,1,0:T(8,128)(2,1)} %bitcast.12), custom_call_target="tpu_custom_call" | custom-call | flops 10871635968 | bytes 16777216 | tf_op jit(solution)/shard_map/pallas_call | solution.py:209
  155.0 0.9 copy.13
  155.9 0.5 copy.14
  156.3 1.2 reshape.19
  (1 shorter events, 0.0 us)
Async XLA Ops:
  3.1 2.0 %copy-start = (s32[1,8]{1,0:T(1,128)S(1)}, s32[1,8]{1,0:T(1,128)}, u32[]{:S(2)}) copy-start(s32[1,8]{1,0:T(1,128)} %param.6) | copy-start | bytes 100

commit v2 on v1

--- a/solution.py
+++ b/solution.py
@@ -10,8 +10,10 @@
 
 VMEM_BYTES = 52 * 2**20
 COLS = 256
+LAG = 2
+EARLY = 4
+OWN_LAG = 1
 MESH = pl.DeviceIdType.MESH
-X_FIRST = 1
 
 
 def select(table, at):
@@ -22,17 +24,17 @@
 
 
 def ladder_kernel(n_occ, n_vir, slot_ref, amp_ref, int_hbm, out_ref,
-                  gath, ints, turn, flip, lad, mir, acc,
+                  gath, ints, turn, flip, lad, mir, acc, pick,
                   int_sem, send_sem, recv_sem, swap_send, swap_recv):
     n_line = n_vir // 2
     n_blocks, cd_max = n_occ, int_hbm.shape[0]
-    rows, k = amp_ref.shape[1:]
+    rows, k = lad.shape[1:]
     width, side = math.isqrt(k), math.isqrt(rows)
     occ, vir = lax.axis_index("occ"), lax.axis_index("vir")
     line, pair = vir // 2, vir % 2
     partner = line * 2 + 1 - pair
 
-    near = [sorted(range(n_line), key=lambda at: (abs(at - here), at)) for here in range(n_line)]
+    near = [sorted(range(n_line), key=lambda at: (abs(at - here), abs(2 * at - n_line + 1))) for here in range(n_line)]
     by_rank = [select([near[here][rank] for here in range(n_line)], line) for rank in range(n_line)]
 
     def block_of(step):
@@ -58,48 +60,71 @@
 
     fetch = pltpu.make_async_copy(int_hbm, ints.at[pl.ds(0, cd_max)], int_sem)
     fetch.start()
-    for step in range(n_blocks):
-        gath[step, vir] = amp_ref[block_of(step)]
+
+    def group(step):
+        at = lax.broadcasted_iota(jnp.int32, (rows, n_blocks * rows), 0)
+        source = lax.broadcasted_iota(jnp.int32, (rows, n_blocks * rows), 1)
+        wanted = (at // side) * (side * n_blocks) + block_of(step) * side + at % side
+        pick[...] = jnp.where(source == wanted, 1.0, 0.0).astype(jnp.bfloat16)
+
+        def part(n, carry):
+            cols = pl.ds(pl.multiple_of(n * COLS, COLS), COLS)
+            gath[step, vir, :, cols] = jnp.dot(
+                pick[...], amp_ref[:, cols], preferred_element_type=jnp.float32).astype(jnp.bfloat16)
+            return carry
+
+        lax.fori_loop(0, k // COLS, part, 0)
+
+    group(0)
     waits = n_occ + jnp.where(line > 0, 1, 0) + jnp.where(line < n_line - 1, 1, 0)
     pl.semaphore_wait(barrier, waits)
 
-    def copies(step, at, own_column):
+    early = max(16, rows // EARLY // 16 * 16)
+    parts = [(0, rows - early), (rows - early, early)]
+
+    def copies(step, at, own_column, part):
         tile = at * 2 + (pair if own_column else 1 - pair)
-        crossed = step == X_FIRST
         up = (at <= line) & (line < n_line - 1)
         down = (at >= line) & (line > 0)
+        plan = []
+        if own_column or part == 1:
+            plan = [(0, up, vir + 2), (1, down, vir - 2)]
         if own_column:
-            across = jnp.logical_not(crossed) | (at == line)
-        else:
-            up, down, across = up & crossed, down & crossed, None
-        plan = [(0, up, vir + 2), (1, down, vir - 2), (2, across, partner)]
+            plan.append((2, at == line if part == 1 else at >= 0, partner))
 
         def copy(way, target):
+            block = gath.at[step, tile, pl.ds(*parts[part])]
             return pltpu.make_async_remote_copy(
-                src_ref=gath.at[step, tile],
-                dst_ref=gath.at[step, tile],
-                send_sem=send_sem.at[way, step, tile],
-                recv_sem=recv_sem.at[step, tile],
-                device_id=(occ, target),
-                device_id_type=MESH,
+                src_ref=block, dst_ref=block,
+                send_sem=send_sem.at[way, part, step, tile],
+                recv_sem=recv_sem.at[part, step, tile],
+                device_id=(occ, target), device_id_type=MESH,
             )
 
-        return [(cond, functools.partial(copy, way, target))
-                for way, cond, target in plan if cond is not None]
-
-    def forward(step, at, own_column):
-        for cond, make in copies(step, at, own_column):
+        return [(cond, functools.partial(copy, way, target)) for way, cond, target in plan]
+
+    def forward(step, at, own_column, part):
+        for cond, make in reversed(copies(step, at, own_column, part)):
             @pl.when(cond)
             def _(make=make):
                 make().start()
 
-    def arrived(step, at, own_column):
+    def send_own(step):
+        forward(step, line, True, 1)
+        forward(step, line, True, 0)
+
+    def arrived(step, at, own_column, part):
         tile = at * 2 + (pair if own_column else 1 - pair)
+        block = gath.at[step, tile, pl.ds(*parts[part])]
         pltpu.make_async_remote_copy(
-            src_ref=gath.at[step, tile], dst_ref=gath.at[step, tile],
-            send_sem=send_sem.at[0, step, tile], recv_sem=recv_sem.at[step, tile],
+            src_ref=block, dst_ref=block,
+            send_sem=send_sem.at[0, part, step, tile], recv_sem=recv_sem.at[part, step, tile],
             device_id=(occ, partner), device_id_type=MESH,
         ).wait_recv()
+
+    def take(step, at, own_column, part):
+        arrived(step, at, own_column, part)
+        forward(step, at, own_column, part)
 
     def product(step, at, own_column, first):
         tile = at * 2 + (pair if own_column else 1 - pair)
@@ -111,9 +136,9 @@
                 gath[step, tile], ints[slot, cols, :], (((1,), (1,)), ((), ())),
                 preferred_element_type=jnp.float32)
             if first:
-                acc[:, cols] = term
+                acc[step % 2, :, cols] = term
             else:
-                acc[:, cols] += term
+                acc[step % 2, :, cols] += term
             return carry
 
         lax.fori_loop(0, k // COLS, part, 0)
@@ -138,9 +163,6 @@
 
         lax.fori_loop(0, k // COLS, part, 0)
 
-    forward(0, line, True)
-    ints[cd_max] = jnp.zeros((k, k), jnp.bfloat16)
-
     def build(n, carry):
         cols = pl.ds(pl.multiple_of(n * COLS, COLS), COLS)
         row = lax.broadcasted_iota(jnp.int32, (k, COLS), 0)
@@ -148,46 +170,58 @@
         turn[:, cols] = jnp.where(row == (col % width) * width + col // width, 1.0, 0.0).astype(jnp.bfloat16)
         return carry
 
-    lax.fori_loop(0, k // COLS, build, 0)
-    row = lax.broadcasted_iota(jnp.int32, (rows, rows), 0)
-    col = lax.broadcasted_iota(jnp.int32, (rows, rows), 1)
-    flip[...] = jnp.where(row == (col % side) * side + col // side, 1.0, 0.0).astype(jnp.bfloat16)
-    fetch.wait()
-
-    order = [(0, True)]
-    for rank in range(1, n_line):
-        order += [(rank, True), (rank - 1, False)]
-    order.append((n_line - 1, False))
-
-    def visit(step, carry):
-        @pl.when(step + 1 < n_blocks)
-        def _():
-            forward(step + 1, line, True)
-
-        for number, (rank, own_column) in enumerate(order):
-            at = by_rank[rank]
-            if number:
-                arrived(step, at, own_column)
-                forward(step, at, own_column)
-            product(step, at, own_column, number == 0)
-        lad[step] = acc[...].astype(jnp.bfloat16)
-        swap(step).start()
-
-        @pl.when(step > 0)
-        def _():
-            finish(step - 1)
-
-        return carry
-
-    lax.fori_loop(0, n_blocks, visit, 0)
+    def along(step, rank):
+        at = by_rank[rank]
+        if rank == 0:
+            if step + 1 < n_blocks:
+                send_own(step + 1)
+        else:
+            take(step, at, True, 0)
+            take(step, at, True, 1)
+        take(step, at, False, 1)
+
+    def own(step, rank):
+        if step == 0 and rank == 0:
+            ints[cd_max] = jnp.zeros((k, k), jnp.bfloat16)
+            fetch.wait()
+        product(step, by_rank[rank], True, rank == 0)
+
+    def across(step, rank):
+        at = by_rank[rank]
+        arrived(step, at, False, 0)
+        product(step, at, False, False)
+        if rank == n_line - 1:
+            lad[step] = acc[step % 2].astype(jnp.bfloat16)
+            swap(step).start()
+
+    send_own(0)
+    for step in range(1, n_blocks):
+        group(step)
+    events = [(step, rank) for step in range(n_blocks) for rank in range(n_line)]
+    for number in range(len(events) + LAG):
+        if number < len(events):
+            along(*events[number])
+        if 0 <= number - OWN_LAG < len(events):
+            own(*events[number - OWN_LAG])
+        if number == 2:
+            lax.fori_loop(0, k // COLS, build, 0)
+            row = lax.broadcasted_iota(jnp.int32, (rows, rows), 0)
+            col = lax.broadcasted_iota(jnp.int32, (rows, rows), 1)
+            flip[...] = jnp.where(row == (col % side) * side + col // side, 1.0, 0.0).astype(jnp.bfloat16)
+        if number >= LAG:
+            step, rank = events[number - LAG]
+            across(step, rank)
+            if step > 0 and rank == n_line - 2:
+                finish(step - 1)
     finish(n_blocks - 1)
 
     def drain(step, carry):
-        for rank, own_column in order:
-            for cond, make in copies(step, by_rank[rank], own_column):
-                @pl.when(cond)
-                def _(make=make):
-                    make().wait_send()
+        for rank in range(n_line):
+            for own_column, part in ((True, 0), (True, 1), (False, 1)):
+                for cond, make in copies(step, by_rank[rank], own_column, part):
+                    @pl.when(cond)
+                    def _(make=make):
+                        make().wait_send()
         swap(step).wait_send()
         return carry
 
@@ -203,12 +237,11 @@
     slots = jnp.arange(cd_max, dtype=jnp.int32)
     hit = (listed[None, :] == jnp.arange(n_vir, dtype=jnp.int32)[:, None]) & (slots < live)[None, :]
     slot_of = jnp.min(jnp.where(hit, slots[None, :], cd_max), axis=1).astype(jnp.int32)
-    blocks = amplitudes.reshape(side, n_occ, side, k).transpose(1, 0, 2, 3).reshape(n_occ, side * side, k)
     block = side * side
     bf16 = jnp.bfloat16
     result = pl.pallas_call(
         functools.partial(ladder_kernel, n_occ, n_vir),
-        out_shape=jax.ShapeDtypeStruct(blocks.shape, bf16),
+        out_shape=jax.ShapeDtypeStruct((n_occ, block, k), bf16),
         in_specs=[
             pl.BlockSpec(memory_space=pltpu.SMEM),
             pl.BlockSpec(memory_space=pltpu.VMEM),
@@ -222,10 +255,11 @@
             pltpu.VMEM((block, block), bf16),
             pltpu.VMEM((n_occ, block, k), bf16),
             pltpu.VMEM((n_occ, block, k), bf16),
-            pltpu.VMEM((block, k), jnp.float32),
+            pltpu.VMEM((2, block, k), jnp.float32),
+            pltpu.VMEM((block, rows), bf16),
             pltpu.SemaphoreType.DMA,
-            pltpu.SemaphoreType.DMA((3, n_occ, n_vir)),
-            pltpu.SemaphoreType.DMA((n_occ, n_vir)),
+            pltpu.SemaphoreType.DMA((3, 2, n_occ, n_vir)),
+            pltpu.SemaphoreType.DMA((2, n_occ, n_vir)),
             pltpu.SemaphoreType.DMA((n_occ,)),
             pltpu.SemaphoreType.DMA((n_occ,)),
         ],
@@ -233,7 +267,7 @@
             collective_id=0, has_side_effects=True, vmem_limit_bytes=VMEM_BYTES),
         cost_estimate=pl.CostEstimate(
             flops=2 * rows * k * k * (n_vir + 1), bytes_accessed=2 * cd_max * k * k, transcendentals=0),
-    )(slot_of, blocks, integrals[0])
+    )(slot_of, amplitudes, integrals[0])
     return result.reshape(n_occ, side, side, k).transpose(1, 0, 2, 3).reshape(rows, k)
 
 

time: 159 us -> 135 us (0.85)
  Pallas kernels: 150 us -> 131 us
  local copies, waits for them, and re-layouts: 6.97 us -> 2.53 us
    pallas_call x1, Pallas kernels: 150 us -> 131 us  [fused(): pl.pallas_call(functools.partial(ladder_kernel, n_occ, n_vir), out_shape=...]
    reshape x2 -> x0, local copies, waits for them, and re-layouts: 3.51 us -> none  [fused(): amplitudes.reshape(side, n_occ, side, k).transpose(1, 0, 2, 3)]
where the time goes in v2:
time: 135 us
  Pallas kernels  131 us (97%)
  local copies, waits for them, and re-layouts  2.53 us (2%)
    pallas_call x1, Pallas kernels, fused(): pl.pallas_call(functools.partial(ladder_kernel, n_occ, n_vir), out_shape=...  131 us

profile of v2, /device:TPU:0, one launch (start us, length us, event | category | flops | bytes accessed | tf_op | source)
XLA Modules:
  0.0 134.9 jit_solution(16547686727179788628)
XLA Ops:
  0.7 0.8 select_reduce_fusion.slot_ref
  1.4 130.9 %shard_map.46 = bf16[4,144,1024]{2,1,0:T(8,128)(2,1)S(1)} custom-call(s32[8]{0:T(128)S(1)} %select_reduce_fusion.slot_ref, bf16[576,1024]{1,0:T(8,128)(2,1)} %amp_ref.1, bf16[8,1024,1024]{2,1,0:T(8,128)(2,1)} %bitcast.8), custom_call_target="tpu_custom_call" | custom-call | flops 10871635968 | bytes 16777216 | tf_op jit(solution)/shard_map/pallas_call | solution.py:242
  132.3 0.9 copy.8
  133.2 0.5 copy.9
  133.7 1.2 reshape.11
  (1 shorter events, 0.0 us)
